TPU v7x, 256 devices: a whole 4x4x8 slice. The times are simulated.
256 devices in a mesh: wide: 32 (over z_lo, x, core), narrow: 8 (over z_hi, y).
Axes of the slice: x: 4, y: 4, z: 8 (z_hi: 2, z_lo: 4; z = z_hi * 4 + z_lo), core: 2. Of those that a mesh axis runs over, the one named last changes fastest.
Arguments:
- hidden_in: bfloat16 [512, 18432], P('narrow', 'wide'), may hold values from -50 to 50
- ln_gain: float32 [18432], P('wide'), may hold values from 0.5 to 1.5
- gate_weight: bfloat16 [18432, 36864], P('wide', 'narrow'), may hold values from -0.046875 to 0.046875
- up_weight: bfloat16 [18432, 36864], P('wide', 'narrow'), may hold values from -0.046875 to 0.046875
- query_weight: bfloat16 [18432, 6144], P('wide', 'narrow'), may hold values from -0.046875 to 0.046875
- kv_weight: bfloat16 [18432, 512], P('wide'), may hold values from -0.046875 to 0.046875
- out_weight: bfloat16 [6144, 18432], P('narrow', 'wide'), may hold values from -0.078125 to 0.078125
- cache_keys: bfloat16 [512, 384, 256], P(('wide', 'narrow')), may hold values from -130 to 130
- cache_values: bfloat16 [512, 384, 256], P(('wide', 'narrow')), may hold values from -24 to 24
- lengths: int32 [512], P(('wide', 'narrow')), may hold values from 1 to 384, 98304 in all
Outputs:
- update: bfloat16 [512, 18432], P('narrow', 'wide')
- slab_hidden: bfloat16 [512, 36864], P('wide', 'narrow')
Inputs may be any that keep to these rules, and one draw needn't show every extreme that they name: `lengths`: the longest request fills all 384 positions in every draw.
All inputs are finite; a program needn't handle non-finite values. No bound on the sum of `lengths` on one device may be relied on, other than what follows from the above.
Results may differ from a plain program's by a relative error of at most 0.012.
Values may be sent and summed in bfloat16 or wider, within the bound.
A program may use at most 128 MiB of HBM per device.

v0:
```python
import jax
import jax.numpy as jnp
from jax import lax
from jax.sharding import PartitionSpec as P

D = 18432


EPS = 1e-05


def attend(query, new_kv, keys, values, lengths):
    requests = query.shape[0]
    head_dim = keys.shape[2]
    heads = query.shape[1] // head_dim
    grouped = query.reshape(requests, heads, head_dim)
    new_key = new_kv[:, :head_dim]
    new_value = new_kv[:, head_dim:]
    factor = 1.0 / head_dim**0.5
    scores = jnp.einsum("rhd,rld->rhl", grouped, keys, preferred_element_type=jnp.float32) * factor
    own_score = (
        jnp.einsum("rhd,rd->rh", grouped, new_key, preferred_element_type=jnp.float32) * factor
    )
    position = lax.broadcasted_iota(jnp.int32, (1, 1, keys.shape[1]), 2)
    usable = position < lengths[:, None, None]
    masked = jnp.where(usable, scores, -1e30)
    highest = jnp.maximum(jnp.max(masked, axis=2), own_score)
    exps = jnp.where(usable, jnp.exp(masked - highest[:, :, None]), 0.0)
    own_exp = jnp.exp(own_score - highest)
    denominator = jnp.sum(exps, axis=2) + own_exp
    cached_weights = (exps / denominator[:, :, None]).astype(jnp.bfloat16)
    own_weight = (own_exp / denominator).astype(jnp.bfloat16)
    context = jnp.einsum("rhl,rld->rhd", cached_weights, values, preferred_element_type=jnp.float32)
    context = (
        context
        + own_weight.astype(jnp.float32)[:, :, None] * new_value.astype(jnp.float32)[:, None, :]
    )
    return context.reshape(requests, heads * head_dim).astype(jnp.bfloat16)


def local(
    hidden_in,
    ln_gain,
    gate_weight,
    up_weight,
    query_weight,
    kv_weight,
    out_weight,
    cache_keys,
    cache_values,
    lengths,
):
    floats = hidden_in.astype(jnp.float32)
    row_sums, row_squares = lax.psum(
        (jnp.sum(floats, axis=1), jnp.sum(floats * floats, axis=1)), "wide"
    )
    row_average = row_sums / D
    row_variance = row_squares / D - row_average * row_average
    normed = (
        (floats - row_average[:, None]) * lax.rsqrt(row_variance[:, None] + EPS) * ln_gain[None, :]
    ).astype(jnp.bfloat16)
    slab_cols = gate_weight.shape[1]
    query_cols = query_weight.shape[1]
    requests = cache_keys.shape[0]
    segment = lax.all_gather(normed, "narrow", axis=0, tiled=True)
    partial_sums = jnp.concatenate(
        [
            jnp.dot(segment, gate_weight, preferred_element_type=jnp.float32),
            jnp.dot(segment, up_weight, preferred_element_type=jnp.float32),
            jnp.dot(segment, query_weight, preferred_element_type=jnp.float32),
            jnp.dot(segment, kv_weight, preferred_element_type=jnp.float32),
        ],
        axis=1,
    )
    own_block = lax.psum_scatter(partial_sums, "wide", scatter_dimension=0, tiled=True)
    slab_hidden = (
        jax.nn.silu(own_block[:, :slab_cols]) * own_block[:, slab_cols : 2 * slab_cols]
    ).astype(jnp.bfloat16)
    query = own_block[:, 2 * slab_cols : 2 * slab_cols + query_cols].astype(jnp.bfloat16)
    kv_block = own_block[:, 2 * slab_cols + query_cols :]
    new_kv = lax.dynamic_slice_in_dim(
        kv_block, lax.axis_index("narrow") * requests, requests, 0
    ).astype(jnp.bfloat16)
    heads_query = lax.all_to_all(query, "narrow", split_axis=0, concat_axis=1, tiled=True)
    context = attend(heads_query, new_kv, cache_keys, cache_values, lengths)
    returned = lax.all_to_all(context, "narrow", split_axis=1, concat_axis=0, tiled=True)
    attention_part = jnp.dot(
        lax.all_gather(returned, "wide", axis=0, tiled=True),
        out_weight,
        preferred_element_type=jnp.float32,
    )
    update = lax.psum_scatter(attention_part, "narrow", scatter_dimension=0, tiled=True)
    return (update.astype(jnp.bfloat16), slab_hidden)


def solution(mesh):
    placed = (
        P("narrow", "wide"),
        P("wide"),
        P("wide", "narrow"),
        P("wide", "narrow"),
        P("wide", "narrow"),
        P("wide", None),
        P("narrow", "wide"),
        P(("wide", "narrow"), None, None),
        P(("wide", "narrow"), None, None),
        P(("wide", "narrow")),
    )
    return jax.shard_map(
        local,
        mesh=mesh,
        in_specs=placed,
        out_specs=(P("narrow", "wide"), P("wide", "narrow")),
        check_vma=False,
    )
```

profile of v0, /device:TPU:1, one launch (start us, length us, event | category | flops | bytes accessed | tf_op | source)
XLA Modules:
  0.0 495.3 jit_solution(7478035892760909972)
XLA Ops:
  7.2 0.0 copy-start
  7.2 0.0 reduce-scatter.3.cloned.1.call-start
  7.2 1.1 convert_reduce_fusion
  8.3 70.1 %all-reduce = (f32[64]{0:T(128)S(1)}, f32[64]{0:T(128)S(1)}) all-reduce(f32[64]{0:T(128)S(1)} %get-tuple-element.3, f32[64]{0:T(128)S(1)} %get-tuple-element.2), channel_id=1, replica_groups=mesh['wide'=32,'narrow'=8] {'wide'}, use_global_device_ids=true, to_apply=%region_3.0 | all-reduce | flops 128 | bytes 1024 | tf_op jit(solution)/shard_map/psum | solution.py:54
  78.4 1.0 fusion.5
  79.4 0.0 slice-start
  79.4 40.3 %all_gather.6 = bf16[512,576]{1,0:T(8,128)(2,1)S(1)} all-gather(bf16[64,576]{1,0:T(8,128)(2,1)S(1)} %fusion.5), channel_id=1, replica_groups=mesh['wide'=32,'narrow'=8] {'narrow'}, dimensions={0}, use_global_device_ids=true | all-gather | bytes 663552 | tf_op jit(solution)/shard_map/all_gather | solution.py:65
  119.7 0.0 slice-start.1
  119.7 5.9 %fusion.18 = f32[512,4608]{1,0:T(8,128)S(1)} fusion(bf16[512,576]{1,0:T(8,128)(2,1)S(1)} %all_gather.6, bf16[576,4608]{1,0:T(8,128)(2,1)} %param.12), kind=kOutput, calls=%fused_computation.37 | convolution fusion | flops 2717908992 | bytes 15335424 | tf_op jit(solution)/shard_map/dot_general | solution.py:68
  125.5 0.0 slice-done
  125.6 0.0 slice-done.1
  125.6 0.0 copy-start.1
  125.6 6.3 %fusion.19 = f32[512,4608]{1,0:T(8,128)} fusion(bf16[512,576]{1,0:T(8,128)(2,1)S(1)} %all_gather.6, bf16[576,4608]{1,0:T(8,128)(2,1)S(1)} %bitcast.25), kind=kOutput, calls=%fused_computation.38 | convolution fusion | flops 2717908992 | bytes 15335424 | tf_op jit(solution)/shard_map/dot_general | solution.py:69
  131.9 0.0 copy-done
  131.9 0.8 fusion.20
  132.6 0.0 copy-done.1
  132.7 0.6 fusion.21
  133.2 11.3 %pad_maximum_fusion = f32[512,10496]{1,0:T(8,128)} fusion(f32[512,512]{1,0:T(8,128)S(1)} %fusion.21, f32[512,768]{1,0:T(8,128)S(1)} %fusion.20, f32[512,4608]{1,0:T(8,128)} %fusion.19, f32[512,4608]{1,0:T(8,128)S(1)} %fusion.18), kind=kLoop, calls=%fused_computation | loop fusion | flops 16121856 | bytes 42991616 | tf_op jit(solution)/shard_map/concatenate | solution.py:66
  144.6 0.0 copy-start.3
  144.6 0.0 copy-start.2
  144.6 0.0 copy-start.5
  144.6 0.0 copy-start.4
  144.6 0.0 reduce-scatter.3.cloned.1.call-update
  144.6 0.6 copy-done.3
  145.2 0.1 iota_compare_fusion
  145.3 181.8 %reduce-scatter.3.cloned.1.call-done = f32[16,10496]{1,0:T(8,128)} async-done(((f32[512,10496]{1,0:T(8,128)}), f32[16,10496]{1,0:T(8,128)}) %reduce-scatter.3.cloned.1.call-update) | async-done | bytes 671760 | tf_op jit(solution)/shard_map/reduce_scatter | solution.py:75
  327.1 0.8 slice.38
  327.9 0.6 all_to_all.24
  328.5 8.2 %all-to-all-start = ((bf16[8,2,768]{2,1,0:T(2,128)(2,1)}), bf16[8,2,768]{2,1,0:T(2,128)(2,1)S(1)}, u32[]{:S(2)}, u32[]{:S(2)}) async-start(bf16[8,2,768]{2,1,0:T(2,128)(2,1)} %all_to_all.24), calls=%async_computation.1 | async-start | bytes 49152 | tf_op jit(solution)/shard_map/all_to_all | solution.py:84
  336.7 0.0 reduce-scatter.5.cloned.1.call-start
  336.8 0.8 slice.26
  337.5 8.2 %all-to-all-done = bf16[8,2,768]{2,1,0:T(2,128)(2,1)S(1)} async-done(((bf16[8,2,768]{2,1,0:T(2,128)(2,1)}), bf16[8,2,768]{2,1,0:T(2,128)(2,1)S(1)}, u32[]{:S(2)}, u32[]{:S(2)}) %all-to-all-start) | async-done | bytes 24608 | tf_op jit(solution)/shard_map/all_to_all | solution.py:84
  345.7 0.1 fusion.12
  345.9 0.0 copy-done.2
  345.9 0.3 fusion.17
  346.2 0.2 fusion.7
  346.4 0.0 copy-done.5
  346.4 0.2 fusion.1
  346.7 11.4 %all_to_all.32 = bf16[2,8,768]{2,0,1:T(2,128)(2,1)S(1)} all-to-all(bf16[2,8,768]{2,0,1:T(2,128)(2,1)S(1)} %copy.16), channel_id=1, replica_groups=mesh['wide'=32,'narrow'=8] {'narrow'}, dimensions={1} | all-to-all | bytes 49152 | tf_op jit(solution)/shard_map/all_to_all | solution.py:86
  358.0 46.7 %all_gather.7 = bf16[512,768]{1,0:T(8,128)(2,1)S(1)} all-gather(bf16[16,768]{1,0:T(8,128)(2,1)S(1)} %all_to_all.29), channel_id=1, replica_groups=mesh['wide'=32,'narrow'=8] {'wide'}, dimensions={0}, use_global_device_ids=true | all-gather | bytes 811008 | tf_op jit(solution)/shard_map/all_gather | solution.py:88
  404.8 0.0 copy-done.4
  404.8 1.9 fusion.22
  406.7 0.0 reduce-scatter.5.cloned.1.call-update
  406.7 1.8 fusion.2
  408.5 78.4 %reduce-scatter.5.cloned.1.call-done = f32[64,576]{1,0:T(8,128)} async-done(((f32[512,576]{1,0:T(8,128)}), f32[64,576]{1,0:T(8,128)}) %reduce-scatter.5.cloned.1.call-update) | async-done | bytes 147472 | tf_op jit(solution)/shard_map/reduce_scatter | solution.py:92
  486.9 1.6 convert_element_type.44
  (11 shorter events, 0.1 us)
Async XLA Ops:
  7.2 124.7 %copy-start = (bf16[576,768]{1,0:T(8,128)(2,1)S(1)}, bf16[576,768]{1,0:T(8,128)(2,1)}, u32[]{:S(2)}) copy-start(bf16[576,768]{1,0:T(8,128)(2,1)} %param.14) | copy-start | bytes 2654212
  7.2 319.9 %reduce-scatter.3.cloned.1.call-start = ((), (), s32[]{:S(2)}) async-start(), calls=%async_computation.4 | async-start | bytes 22167552 | tf_op jit(solution)/shard_map/reduce_scatter | solution.py:75
  79.4 46.2 %slice-start = ((s8[5308416]{0:T(1024)(128)(4,1)}), s8[4194304]{0:T(1024)(128)(4,1)S(1)}, s32[]{:S(2)}) async-start(s8[5308416]{0:T(1024)(128)(4,1)} %bitcast.24), calls=%async_computation.6 | async-start | bytes 8388608
  119.7 5.9 %slice-start.1 = ((s8[5308416]{0:T(1024)(128)(4,1)}), s8[1114112]{0:T(1024)(128)(4,1)S(1)}, s32[]{:S(2)}) async-start(s8[5308416]{0:T(1024)(128)(4,1)} %bitcast.24), calls=%async_computation.7 | async-start | bytes 2228224
  125.6 7.1 %copy-start.1 = (bf16[576,512]{1,0:T(8,128)(2,1)S(1)}, bf16[576,512]{1,0:T(8,128)(2,1)}, u32[]{:S(2)}) copy-start(bf16[576,512]{1,0:T(8,128)(2,1)} %param.15) | copy-start | bytes 1769476
  144.6 0.7 copy-start.3
  144.6 201.3 %copy-start.2 = (bf16[2,384,256]{2,1,0:T(8,128)(2,1)S(1)}, bf16[2,384,256]{2,1,0:T(8,128)(2,1)}, u32[]{:S(2)}) copy-start(bf16[2,384,256]{2,1,0:T(8,128)(2,1)} %param.17) | copy-start | bytes 1179652
  144.6 201.8 %copy-start.5 = (bf16[2,384,256]{2,1,0:T(8,128)(2,1)S(1)}, bf16[2,384,256]{2,1,0:T(8,128)(2,1)}, u32[]{:S(2)}) copy-start(bf16[2,384,256]{2,1,0:T(8,128)(2,1)} %param.18) | copy-start | bytes 1179652
  144.6 260.2 %copy-start.4 = (bf16[768,576]{0,1:T(8,128)(2,1)S(1)}, bf16[768,576]{0,1:T(8,128)(2,1)}, u32[]{:S(2)}) copy-start(bf16[768,576]{0,1:T(8,128)(2,1)} %param.16) | copy-start | bytes 2654212
  328.5 17.2 %all-to-all-start = ((bf16[8,2,768]{2,1,0:T(2,128)(2,1)}), bf16[8,2,768]{2,1,0:T(2,128)(2,1)S(1)}, u32[]{:S(2)}, u32[]{:S(2)}) async-start(bf16[8,2,768]{2,1,0:T(2,128)(2,1)} %all_to_all.24), calls=%async_computation.1 | async-start | bytes 49152 | tf_op jit(solution)/shard_map/all_to_all | solution.py:84
  336.7 150.2 %reduce-scatter.5.cloned.1.call-start = ((), (), s32[]{:S(2)}) async-start(), calls=%async_computation.5 | async-start | bytes 1474560 | tf_op jit(solution)/shard_map/reduce_scatter | solution.py:92
Sparse Core Ops, SparseCore 0:
  144.7 182.3 reduce-scatter.2
  406.8 80.0 reduce-scatter.4
where the time goes:
time: 496 us; the launch traced here: 495 us
  waiting for transfers between devices  268 us (54%)
  blocking collectives  168 us (34%)
  other arithmetic  17.1 us (3%)
  matrix products  16 us (3%)
  between operations  14.2 us (3%)
  starting transfers between devices  8.24 us (2%)
    reduce_scatter x1, waiting for transfers between devices, local(): lax.psum_scatter(partial_sums, 'wide', scatter_dimension=0, tiled=True)  182 us
    reduce_scatter x1, waiting for transfers between devices, local(): lax.psum_scatter(attention_part, 'narrow', scatter_dimension=0, tiled=True)  78.4 us
    psum x1, blocking collectives, local(): lax.psum((jnp.sum(floats, axis=1), jnp.sum(floats * floats, axis=1)), 'wi...  70.1 us
    all_gather x1, blocking collectives, local(): lax.all_gather(returned, 'wide', axis=0, tiled=True)  46.7 us
    all_gather x1, blocking collectives, local(): segment = lax.all_gather(normed, 'narrow', axis=0, tiled=True)  40.3 us
    all_to_all x1, blocking collectives, local(): lax.all_to_all(context, 'narrow', split_axis=1, concat_axis=0, tiled=True)  11.4 us
    concatenate x1, other arithmetic, local(): jnp.concatenate([jnp.dot(segment, gate_weight, preferred_element_type=jnp...  11.3 us
  transfers between devices with their start and end apart: 3, of which 3 were waited for; matrix products, arithmetic and copies ran while one was open for 1% of the time, Pallas kernels for 0%

commit v1 on v0

v1 whole, which is shorter than its diff:
```python
import functools

import jax
import jax.numpy as jnp
from jax import lax
from jax.experimental import pallas as pl
from jax.experimental.pallas import tpu as pltpu
from jax.sharding import PartitionSpec as P

D = 18432
EPS = 1e-05
MESH = pl.DeviceIdType.MESH
F32 = jnp.float32
BF16 = jnp.bfloat16
KB = 576
KP = 640
CHUNKS = 9
CW = 256
HALF = CHUNKS * CW

STEP = dict(Q1=2, Q2=5, Q3=6, Q4=7, C1=9, C2=10, C3=12, C4=13, C5=15)
LAG1, LAG2, LAG3 = 2, 4, 6
STEPS = 16


def device(x, y, zl, zh, c):
    return ((zl * 4 + x) * 2 + c, zh * 4 + y)


def kernel(
    hidden,
    gain,
    gate_w,
    up_w,
    query_w,
    kv_w,
    out_w,
    keys_h,
    values_h,
    lengths,
    update,
    slab,
    raw,
    normed,
    gains,
    wgu,
    wq,
    wkv,
    wo,
    keys,
    values,
    cst,
    zst,
    xst,
    yst,
    part,
    r1,
    s1,
    r2,
    zs,
    zr,
    sl,
    sr,
    kvs,
    pq,
    rq,
    zq,
    zqr,
    cx,
    cxr,
    yt,
    yr,
    q48,
    ctx,
    caf,
    ca,
    ar,
    bs,
    br,
    brf,
    ctf,
    ct,
    os_,
    or_,
    vf,
    fs,
    fr,
    lsem,
    wS, wR, gS, gR, rawS, rawR, sibS, sibR,
    cstS, cstR, zstS, zstR, xstS, xstR, ystS, ystR,
    r1S, r1R, r2S, r2R, zS, zR, slS, slR,
    qxS, qxR, qzS, qzR, qcS, qcR, qyS, qyR,
    aS, aR, bS, bR, cS, cR, dS, dR, eS, eR, fS, fR,
):
    w = lax.axis_index("wide")
    n = lax.axis_index("narrow")
    c = lax.rem(w, 2)
    x = lax.rem(w // 2, 4)
    zl = w // 8
    zh = n // 4
    y = lax.rem(n, 4)
    z = zh * 4 + zl
    sib = device(x, y, zl, zh, 1 - c)
    partner = device(x, y, zl, 1 - zh, c)

    def on_x(p):
        return device(p, y, zl, zh, c)

    def on_y(p):
        return device(x, p, zl, zh, c)

    def on_z(p):
        return device(x, y, lax.rem(p, 4), p // 4, c)

    def remote(src, dst, ss, rs, to):
        return pltpu.make_async_remote_copy(
            src_ref=src, dst_ref=dst, send_sem=ss, recv_sem=rs, device_id=to, device_id_type=MESH
        )

    drains = {}

    def start(name, args):
        remote(*args()).start()
        drains[name] = lambda: remote(*args()).wait_send()

    def arrived(dst, ss, rs):
        remote(dst, dst, ss, rs, sib).wait_recv()

    def peers(me, size):
        return [(d, lax.rem(me + d, size)) for d in range(1, size)]

    on_x.peers, on_y.peers, on_z.peers = peers(x, 4), peers(y, 4), peers(z, 8)
    zl_peers = peers(zl, 4)

    def spread(name, src, dst, ss, rs, me, on):
        for d, p in on.peers:
            start(name + str(d), lambda d=d, p=p: (src(p), dst.at[me], ss.at[d], rs.at[me], on(p)))

    def collect(dst, ss, rs, on):
        for d, p in on.peers:
            arrived(dst.at[p], ss.at[d], rs.at[p])

    half = pl.multiple_of(c * HALF, 128)
    other = pl.multiple_of((1 - c) * HALF, 128)
    mine = pl.ds(pl.multiple_of(c * KP, 128), KB)

    def local(src, dst, i):
        return pltpu.make_async_copy(src, dst, lsem.at[i])

    load_x = local(hidden, raw.at[c, n], 0)
    load_x.start()
    load_q = local(query_w.at[:, pl.ds(pl.multiple_of(c * 384, 128), 384)], wq.at[mine], 1)
    load_kv = local(kv_w.at[:, pl.ds(pl.multiple_of(c * 256, 128), 256)], wkv.at[mine], 2)
    load_o = local(out_w, wo, 3)
    load_k = local(keys_h, keys, 4)
    load_v = local(values_h, values, 5)
    load_q.start()
    load_kv.start()

    def load_gu(j, k):
        src = (gate_w, up_w)[k].at[:, pl.ds(pl.multiple_of(half + j * CW, 128), CW)]
        return local(src, wgu.at[j, mine, pl.ds(k * CW, CW)], 6 + 2 * j + k)

    def send_gu(j, k):
        src = (gate_w, up_w)[k].at[:, pl.ds(pl.multiple_of(other + j * CW, 128), CW)]
        i = 2 + 2 * j + k
        return remote(src, wgu.at[j, mine, pl.ds(k * CW, CW)], wS.at[i], wR.at[i], sib)

    barrier = pltpu.get_barrier_semaphore()
    greeted = (
        [sib]
        + [on_x(p) for _, p in on_x.peers]
        + [on_y(p) for _, p in on_y.peers]
        + [on_z(p) for _, p in on_z.peers]
    )
    for to in greeted:
        pl.semaphore_signal(barrier, inc=1, device_id=to, device_id_type=MESH)

    load_x.wait()
    own = raw[c, n].astype(F32)
    lane = lax.broadcasted_iota(jnp.int32, (64, 128), 1)
    cst[c] = jnp.where(
        lane < 64,
        jnp.sum(own, axis=1, keepdims=True),
        jnp.sum(own * own, axis=1, keepdims=True),
    )
    g8 = jnp.broadcast_to(gain[...], (8, KB))
    gains[c] = g8

    pl.semaphore_wait(barrier, len(greeted))

    start("b11", lambda: (cst.at[c], cst.at[c], cstS.at[0], cstR.at[0], sib))
    for d, p in on_y.peers:
        start("b12_" + str(d), lambda d=d, p=p: (raw.at[c, n], raw.at[c, n], rawS.at[d], rawR.at[n], on_y(p)))
    start("b13", lambda: (raw.at[c, n], raw.at[c, n], rawS.at[0], rawR.at[n], partner))
    start("b14", lambda: (gains.at[c], gains.at[c], gS.at[0], gR.at[0], sib))
    away_q = pl.ds(pl.multiple_of((1 - c) * 384, 128), 384)
    away_kv = pl.ds(pl.multiple_of((1 - c) * 256, 128), 256)
    start("wq", lambda: (query_w.at[:, away_q], wq.at[mine], wS.at[0], wR.at[0], sib))
    start("wkv", lambda: (kv_w.at[:, away_kv], wkv.at[mine], wS.at[1], wR.at[1], sib))

    arrived(cst.at[1 - c], cstS.at[0], cstR.at[0])
    zst[z] = cst[0] + cst[1]
    spread("a01_", lambda p: zst.at[z], zst, zstS, zstR, z, on_z)

    def start_weights(j, carry):
        for k in range(2):
            send_gu(j, k).start()
            load_gu(j, k).start()
        return carry

    lax.fori_loop(0, CHUNKS, start_weights, 0)
    load_o.start()
    load_k.start()
    load_v.start()

    for k in range(2):
        pad = pl.ds(k * KP + KB, KP - KB)
        normed[:, pad] = jnp.zeros((512, KP - KB), BF16)
        wq[pad, :] = jnp.zeros((KP - KB, 384), BF16)
        wkv[pad, :] = jnp.zeros((KP - KB, 256), BF16)

        def fill(j, carry, pad=pad):
            wgu[j, pad, :] = jnp.zeros((KP - KB, 2 * CW), BF16)
            return carry

        lax.fori_loop(0, CHUNKS, fill, 0)
    pq[:, :, 32:40, :] = jnp.zeros((4, 4, 8, 384), F32)
    caf[...] = jnp.zeros((2, 32, 256), F32)

    far = (1 - zh) * 4 + y
    arrived(raw.at[c, far], rawS.at[0], rawR.at[far])
    for d, p in on_y.peers:
        start("b15_" + str(d), lambda d=d, p=p: (raw.at[c, far], raw.at[c, far], rawS.at[3 + d], rawR.at[far], on_y(p)))
    collect(zst, zstS, zstR, on_z)
    for k in range(2):
        xst[x, k] = (zst[4 * k] + zst[4 * k + 1]) + (zst[4 * k + 2] + zst[4 * k + 3])
    spread("a02_", lambda p: xst.at[x], xst, xstS, xstR, x, on_x)
    for d, p in on_y.peers:
        arrived(raw.at[c, zh * 4 + p], rawS.at[d], rawR.at[zh * 4 + p])
    near4 = pl.ds(zh * 4, 4)
    far4 = pl.ds((1 - zh) * 4, 4)
    start("b16", lambda: (raw.at[c, near4], raw.at[c, near4], sibS.at[0], sibR.at[0], sib))
    collect(xst, xstS, xstR, on_x)
    yst[y] = (xst[0] + xst[1]) + (xst[2] + xst[3])
    spread("a03_", lambda p: yst.at[y], yst, ystS, ystR, y, on_y)
    for d, p in on_y.peers:
        arrived(raw.at[c, (1 - zh) * 4 + p], rawS.at[3 + d], rawR.at[(1 - zh) * 4 + p])
    start("b17", lambda: (raw.at[c, far4], raw.at[c, far4], sibS.at[1], sibR.at[1], sib))
    arrived(gains.at[1 - c], gS.at[0], gR.at[0])
    collect(yst, ystS, ystR, on_y)
    arrived(raw.at[1 - c, near4], sibS.at[0], sibR.at[0])
    arrived(raw.at[1 - c, far4], sibS.at[1], sibR.at[1])

    def norm(b, carry):
        stat = yst[lax.rem(b, 4), b // 4]
        average = stat[:, 0:1] / D
        variance = stat[:, 64:65] / D - average * average
        scale = lax.rsqrt(variance + EPS)
        rows = pl.ds(pl.multiple_of(b * 64, 64), 64)
        for k in range(2):
            block = (raw[k, b].astype(F32) - average) * scale * gains[k, 0:1, :]
            normed[rows, k * KP : k * KP + KB] = block.astype(BF16)
        return carry

    lax.fori_loop(0, 8, norm, 0)

    load_q.wait()
    load_kv.wait()
    arrived(wq.at[mine], wS.at[0], wR.at[0])
    arrived(wkv.at[mine], wS.at[1], wR.at[1])
    query = jnp.dot(normed[...], wq[...], preferred_element_type=F32)
    for zz in range(4):
        for xx in range(4):
            at = zz * 128 + xx * 32
            pq[xx, zz, 0:32, :] = query[at : at + 32]
    k64 = lax.broadcasted_iota(jnp.int32, (64, 512), 0)
    r512 = lax.broadcasted_iota(jnp.int32, (64, 512), 1)
    pick = r512 == (k64 >> 1) * 16 + n * 2 + (k64 & 1)
    chosen = jnp.dot(
        jnp.where(pick, 1.0, 0.0).astype(BF16), normed[...], preferred_element_type=F32
    ).astype(BF16)
    kvs[...] = jnp.dot(chosen, wkv[...], preferred_element_type=F32)
    for zz in range(4):
        for xx in range(4):
            at = zz * 16 + xx * 4
            pq[xx, zz, 32:36, 0:256] = kvs[at : at + 4, :]
    spread("a04_", lambda p: pq.at[p], rq, qxS, qxR, x, on_x)

    def part_q1():
        collect(rq, qxS, qxR, on_x)
        total = pq[x]
        for _, p in on_x.peers:
            total = total + rq[p]
        for zz in range(4):
            for hh in range(2):
                to = hh * 4 + zz
                zq[to, 0:8] = total[zz, hh * 8 : hh * 8 + 8]
                zq[to, 8:16] = total[zz, 16 + hh * 8 : 24 + hh * 8]
                zq[to, 16:24] = total[zz, 32:40]
        zqr[z] = zq[z]
        spread("a05_", lambda p: zq.at[p], zqr, qzS, qzR, z, on_z)

    def part_q2():
        collect(zqr, qzS, qzR, on_z)
        sums = [(zqr[k] + zqr[k + 1]) + (zqr[k + 2] + zqr[k + 3]) for k in (0, 4)]
        new = jnp.where(zh == 0, sums[0][16:24], sums[1][16:24])
        for cc in range(2):
            cx[cc, 0:8] = sums[0][cc * 8 : cc * 8 + 8]
            cx[cc, 8:16] = sums[1][cc * 8 : cc * 8 + 8]
            cx[cc, 16:24] = new
        cxr[c] = cx[c]
        start("b18", lambda: (cx.at[1 - c], cxr.at[c], qcS.at[0], qcR.at[0], sib))

    def part_q3():
        arrived(cxr.at[1 - c], qcS.at[0], qcR.at[0])
        for yy in range(4):
            for cs in range(2):
                for hs in range(2):
                    at = hs * 8 + yy * 2
                    yt[yy, cs * 4 + hs * 2 : cs * 4 + hs * 2 + 2, :] = cxr[cs, at : at + 2, :]
        yr[y] = yt[y]
        spread("a06_", lambda p: yt.at[p], yr, qyS, qyR, y, on_y)

    def part_q4():
        collect(yr, qyS, qyR, on_y)
        for yy in range(4):
            at = yy * 4
            q48[at : at + 4, :] = yr[yy, 0:4, 0:256]
            q48[16 + at : 20 + at, 0:128] = yr[yy, 0:4, 256:384]
            q48[16 + at : 20 + at, 128:256] = yr[yy, 4:8, 0:128]
            q48[32 + at : 36 + at, :] = yr[yy, 4:8, 128:384]
        load_k.wait()
        load_v.wait()
        q = q48[...].astype(BF16)
        factor = 1.0 / 16.0
        first = lax.broadcasted_iota(jnp.int32, (48, 1), 0) % 2 == 0

        def fresh(k):
            pair = jnp.where(c == 0, cxr[k, 16:18, 0:256], cxr[k, 18:20, 0:256])
            pair = pair.astype(BF16).astype(F32)
            return jnp.where(first, pair[0:1, :], pair[1:2, :])

        def scores_of(r):
            return lax.dot_general(q, keys[r], (((1,), (1,)), ((), ())), preferred_element_type=F32)

        scores = jnp.where(first, scores_of(0), scores_of(1)) * factor
        own_score = jnp.sum(q.astype(F32) * fresh(0), axis=1, keepdims=True) * factor
        position = lax.broadcasted_iota(jnp.int32, (48, 384), 1)
        usable = position < jnp.where(first, lengths[0], lengths[1])
        masked = jnp.where(usable, scores, -1e30)
        highest = jnp.maximum(jnp.max(masked, axis=1, keepdims=True), own_score)
        exps = jnp.where(usable, jnp.exp(masked - highest), 0.0)
        own_exp = jnp.exp(own_score - highest)
        denominator = jnp.sum(exps, axis=1, keepdims=True) + own_exp
        weights = (exps / denominator).astype(BF16)
        own_weight = (own_exp / denominator).astype(BF16).astype(F32)

        def mixed(r):
            return jnp.dot(weights, values[r], preferred_element_type=F32)

        context = jnp.where(first, mixed(0), mixed(1)) + own_weight * fresh(1)
        ctx[...] = context
        for t in range(3):
            for yy in range(4):
                for hh in range(2):
                    at = t * 16 + yy * 4 + hh * 2
                    caf[hh, yy * 8 + t * 2 : yy * 8 + t * 2 + 2, :] = ctx[at : at + 2, :]
        ca[...] = caf[...].astype(BF16)
        ar[z] = ca[zh]
        spread("a07_", lambda p: ca.at[p // 4], ar, aS, aR, z, on_z)

    def part_c1():
        collect(ar, aS, aR, on_z)
        for yy in range(4):
            bs[yy] = ar[:, yy * 8 : yy * 8 + 8, :].astype(F32).reshape(64, 256).astype(BF16)
        br[y] = bs[y]
        spread("a08_", lambda p: bs.at[p], br, bS, bR, y, on_y)

    def part_c2():
        collect(br, bS, bR, on_y)
        brf[...] = br[...].astype(F32)
        for t in range(3):
            for zz in range(4):
                for hh in range(2):
                    for yy in range(4):
                        to = zz * 16 + hh * 8 + yy * 2
                        at = (hh * 4 + zz) * 8 + t * 2
                        ctf[to : to + 2, t * 256 : t * 256 + 256] = brf[yy, at : at + 2, :]
        ct[c, x] = ctf[...].astype(BF16)
        for d, p in on_x.peers:
            start("b19_" + str(d), lambda d=d, p=p: (ct.at[c, x], ct.at[c, x], cS.at[d], cR.at[x], on_x(p)))
        start("b20", lambda: (ct.at[c, x], ct.at[c, x], dS.at[0], dR.at[x], sib))

    def part_c3():
        for d, p in on_x.peers:
            arrived(ct.at[c, p], cS.at[d], cR.at[p])
            start("b21_" + str(d), lambda d=d, p=p: (ct.at[c, p], ct.at[c, p], dS.at[d], dR.at[p], sib))

    def part_c4():
        load_o.wait()
        for p in range(4):
            arrived(ct.at[1 - c, p], dS.at[p], dR.at[p])
        out = jnp.dot(ct[...].reshape(512, 768), wo[...], preferred_element_type=F32)
        for cc in range(2):
            for xx in range(4):
                for zz in range(4):
                    at = cc * 256 + xx * 64 + zz * 16
                    to = (xx % 2) * 32 + cc * 16
                    os_[(zz % 2) * 2 + xx // 2, zz // 2, to : to + 16, :] = out[at : at + 16].astype(
                        BF16
                    )
        spread("a09_", lambda p: os_.at[p], or_, eS, eR, y, on_y)

    def part_c5():
        collect(or_, eS, eR, on_y)
        total = os_[y].astype(F32)
        for _, p in on_y.peers:
            total = total + or_[p].astype(F32)
        vf[...] = total
        fs[...] = total.astype(BF16)
        start("b22", lambda: (fs.at[1 - zh], fr, fS.at[0], fR.at[0], partner))

    right, left = lax.rem(x + 1, 4), lax.rem(x + 3, 4)
    across = lax.rem(x + 2, 4)

    def first_copies(j):
        return [
            remote(
                part.at[j, :, across, :, pl.ds(k * CW, CW)],
                r1.at[j, k], r1S.at[j, k], r1R.at[j, k], on_x(to),
            )
            for k, to in enumerate((right, left))
        ]

    def second_copies(j):
        return [
            remote(s1.at[j, k], r2.at[j, k], r2S.at[j, k], r2R.at[j, k], on_x(to))
            for k, to in enumerate((right, left))
        ]

    def third_copies(j):
        return [
            remote(zs.at[j, p], zr.at[j, zl], zS.at[j, d], zR.at[j, zl], device(x, y, p, zh, c))
            for d, p in zl_peers
        ]

    def last_copy(j):
        return remote(sl.at[j, 1 - c], sr.at[j], slS.at[j], slR.at[j], sib)

    def multiply(j):
        for k in range(2):
            load_gu(j, k).wait()
            send_gu(j, k).wait_recv()
        product = jnp.dot(normed[...], wgu[j], preferred_element_type=F32)
        part[j] = product.astype(BF16).reshape(4, 4, 32, 2 * CW)
        for copy in first_copies(j):
            copy.start()

    def add_first(j):
        for copy in first_copies(j):
            copy.wait_recv()
        for k, to in enumerate((right, left)):
            for m in range(2):
                cols = slice(m * CW, m * CW + CW)
                if m == k:
                    total = part[j, :, to, :, cols].astype(F32) + r1[j, k].astype(F32)
                    s1[j, k, :, :, cols] = total.astype(BF16)
                else:
                    s1[j, k, :, :, cols] = part[j, :, to, :, cols]
        for copy in second_copies(j):
            copy.start()

    def add_second(j):
        for copy in second_copies(j):
            copy.wait_recv()
        total = part[j, :, x].astype(F32) + r2[j, 0].astype(F32) + r2[j, 1].astype(F32)
        zs[j] = total.astype(BF16)
        for copy in third_copies(j):
            copy.start()

    def finish(j):
        for d, p in zl_peers:
            arrived(zr.at[j, p], zS.at[j, d], zR.at[j, p])
        total = zs[j, zl].astype(F32)
        for _, p in zl_peers:
            total = total + zr[j, p].astype(F32)
        g = total[:, :CW]
        hidden_units = (g * (1.0 / (1.0 + jnp.exp(-g))) * total[:, CW:]).astype(BF16)
        sl[j] = hidden_units.reshape(2, 16, CW)
        last_copy(j).start()
        slab[:, pl.ds(pl.multiple_of(half + j * CW, 128), CW)] = sl[j, c]

    parts = dict(
        Q1=part_q1, Q2=part_q2, Q3=part_q3, Q4=part_q4,
        C1=part_c1, C2=part_c2, C3=part_c3, C4=part_c4, C5=part_c5,
    )

    def step(k, carry):
        for name, run in parts.items():
            pl.when(k == STEP[name])(run)
        for lag, run in ((LAG3, finish), (LAG2, add_second), (LAG1, add_first), (0, multiply)):
            j = k - lag
            pl.when(jnp.logical_and(j >= 0, j < CHUNKS))(functools.partial(run, j))
        return carry

    lax.fori_loop(0, STEPS, step, 0)

    def rest(j, carry):
        last_copy(j).wait_recv()
        slab[:, pl.ds(pl.multiple_of(other + j * CW, 128), CW)] = sr[j]
        for copy in first_copies(j) + second_copies(j) + third_copies(j) + [last_copy(j)]:
            copy.wait_send()
        for k in range(2):
            send_gu(j, k).wait_send()
        return carry

    lax.fori_loop(0, CHUNKS, rest, 0)
    arrived(fr, fS.at[0], fR.at[0])
    update[...] = (vf[zh] + fr[...].astype(F32)).astype(BF16)
    for drain in drains.values():
        drain()


def scratch():
    v = pltpu.VMEM
    s = lambda *shape: pltpu.SemaphoreType.DMA(shape)
    buffers = [
        v((2, 8, 64, KB), BF16),
        v((512, 2 * KP), BF16),
        v((2, 8, KB), F32),
        v((CHUNKS, 2 * KP, 2 * CW), BF16),
        v((2 * KP, 384), BF16),
        v((2 * KP, 256), BF16),
        v((768, KB), BF16),
        v((2, 384, 256), BF16),
        v((2, 384, 256), BF16),
        v((2, 64, 128), F32),
        v((8, 64, 128), F32),
        v((4, 2, 64, 128), F32),
        v((4, 2, 64, 128), F32),
        v((CHUNKS, 4, 4, 32, 2 * CW), BF16),
        v((CHUNKS, 2, 4, 32, CW), BF16),
        v((CHUNKS, 2, 4, 32, 2 * CW), BF16),
        v((CHUNKS, 2, 4, 32, 2 * CW), BF16),
        v((CHUNKS, 4, 32, 2 * CW), BF16),
        v((CHUNKS, 4, 32, 2 * CW), BF16),
        v((CHUNKS, 2, 16, CW), BF16),
        v((CHUNKS, 16, CW), BF16),
        v((64, 256), F32),
        v((4, 4, 40, 384), F32),
        v((4, 4, 40, 384), F32),
        v((8, 24, 384), F32),
        v((8, 24, 384), F32),
        v((2, 24, 384), F32),
        v((2, 24, 384), F32),
        v((4, 8, 384), F32),
        v((4, 8, 384), F32),
        v((48, 256), F32),
        v((48, 256), F32),
        v((2, 32, 256), F32),
        v((2, 32, 256), BF16),
        v((8, 32, 256), BF16),
        v((4, 64, 256), BF16),
        v((4, 64, 256), BF16),
        v((4, 64, 256), F32),
        v((64, 768), F32),
        v((2, 4, 64, 768), BF16),
        v((4, 2, 64, KB), BF16),
        v((4, 2, 64, KB), BF16),
        v((2, 64, KB), F32),
        v((2, 64, KB), BF16),
        v((64, KB), BF16),
    ]
    pair = lambda *shape: [s(*shape), s(*shape)]
    sems = [s(6 + 2 * CHUNKS)]
    sems += pair(2 + 2 * CHUNKS) + pair(1) + [s(7), s(8)] + pair(2)
    sems += pair(1) + pair(8) + pair(4) + pair(4)
    sems += pair(CHUNKS, 2) + pair(CHUNKS, 2) + pair(CHUNKS, 4) + pair(CHUNKS)
    sems += pair(4) + pair(8) + pair(1) + pair(4)
    sems += pair(8) + pair(4) + pair(4) + pair(4) + pair(4) + pair(1)
    return buffers + sems


def local(hidden, gain, *rest):
    anywhere = pl.BlockSpec(memory_space=pl.ANY)
    vmem = pl.BlockSpec(memory_space=pltpu.VMEM)
    return pl.pallas_call(
        kernel,
        out_shape=(
            jax.ShapeDtypeStruct((64, KB), BF16),
            jax.ShapeDtypeStruct((16, 2 * HALF), BF16),
        ),
        in_specs=[anywhere, vmem] + [anywhere] * 7 + [pl.BlockSpec(memory_space=pltpu.SMEM)],
        out_specs=(vmem, vmem),
        scratch_shapes=scratch(),
        compiler_params=pltpu.CompilerParams(
            collective_id=0, has_side_effects=True, vmem_limit_bytes=58 * 1024 * 1024
        ),
        name="layer",
    )(hidden, gain.reshape(1, KB), *rest)


def solution(mesh):
    placed = (
        P("narrow", "wide"),
        P("wide"),
        P("wide", "narrow"),
        P("wide", "narrow"),
        P("wide", "narrow"),
        P("wide", None),
        P("narrow", "wide"),
        P(("wide", "narrow"), None, None),
        P(("wide", "narrow"), None, None),
        P(("wide", "narrow")),
    )
    return jax.shard_map(
        local,
        mesh=mesh,
        in_specs=placed,
        out_specs=(P("narrow", "wide"), P("wide", "narrow")),
        check_vma=False,
    )
```

time: 496 us -> 119 us (0.24)
  waiting for transfers between devices: 268 us -> 0 us
  blocking collectives: 168 us -> 0 us
  Pallas kernels: 0 us -> 111 us
  other arithmetic: 17.1 us -> 0 us
  matrix products: 16 us -> 0 us
  between operations: 14.2 us -> 0.64 us
  starting transfers between devices: 8.24 us -> 0 us
    reduce_scatter x2 -> x0, waiting for transfers between devices: 260 us -> none  [the longest x1 182 us: local(): lax.psum_scatter(partial_sums, 'wide', scatter_dimension=0, tiled=True)]
    pallas_call x0 -> x1, Pallas kernels: none -> 111 us  [local(): pl.pallas_call(kernel, out_shape=(jax.ShapeDtypeStruct((64, KB), BF16), j...]
    all_gather x2 -> x0, blocking collectives: 87 us -> none  [the longest x1 46.7 us: local(): lax.all_gather(returned, 'wide', axis=0, tiled=True)]
    psum x1 -> x0, blocking collectives: 70.1 us -> none  [local(): lax.psum((jnp.sum(floats, axis=1), jnp.sum(floats * floats, axis=1)), 'wi...]
    dot_general x8 -> x0, matrix products: 16 us -> none  [the longest x1 6.27 us: local(): jnp.dot(segment, up_weight, preferred_element_type=jnp.float32)]
    all_to_all x1 -> x0, blocking collectives: 11.4 us -> none  [local(): lax.all_to_all(context, 'narrow', split_axis=1, concat_axis=0, tiled=True)]
    concatenate x1 -> x0, other arithmetic: 11.3 us -> none  [local(): jnp.concatenate([jnp.dot(segment, gate_weight, preferred_element_type=jnp...]
    all_to_all x1 -> x0, starting transfers between devices: 8.17 us -> none  [local(): lax.all_to_all(query, 'narrow', split_axis=0, concat_axis=1, tiled=True)]
  transfers between devices with their start and end apart: 3 -> 0, of which waited for: 3 -> 0; matrix products, arithmetic and copies ran while one was open for 1% -> 0% of each run, Pallas kernels for 0% -> 0%
where the time goes in v1:
time: 119 us
  Pallas kernels  111 us (93%)
  local copies, waits for them, and re-layouts  6.6 us (6%)
    pallas_call x1, Pallas kernels, local(): pl.pallas_call(kernel, out_shape=(jax.ShapeDtypeStruct((64, KB), BF16), j...  111 us
    unnamed x3, local copies, waits for them, and re-layouts  5.34 us

profile of v1, /device:TPU:1, one launch (start us, length us, event | category | flops | bytes accessed | tf_op | source)
XLA Modules:
  0.0 118.7 jit_solution(4923255911315321356)
XLA Ops:
  0.6 1.3 %reshape.7.gain = f32[1,576]{1,0:T(1,128)} reshape(f32[576]{0:T(1024)} %param.11) | data formatting | bytes 4608 | tf_op jit(solution)/shard_map/reshape | solution.py:601
  1.9 2.2 %copy.12.out_w = bf16[768,576]{1,0:T(8,128)(2,1)} copy(bf16[768,576]{0,1:T(8,128)(2,1)} %param.16) | data formatting | bytes 1769472 | tf_op args[6]
  4.1 111.4 %layer.1 = (bf16[64,576]{1,0:T(8,128)(2,1)}, bf16[16,4608]{1,0:T(8,128)(2,1)}) custom-call(bf16[64,576]{1,0:T(8,128)(2,1)} %hidden.1, f32[1,576]{1,0:T(1,128)} %reshape.7.gain, bf16[576,4608]{1,0:T(8,128)(2,1)} %gate_w.1, bf16[576,4608]{1,0:T(8,128)(2,1)} %up_w.1, bf16[576,768]{1,0:T(8,128)(2,1)} %query_w.1, bf16[576,512]{1,0:T(8,128)(2,1)} %kv_w.1, ...), custom_call_target="tpu_custom_call" | custom-call | tf_op jit(solution)/shard_map/layer/pallas_call | solution.py:588
  115.6 1.5 %copy.15 = bf16[64,576]{1,0:T(8,128)(2,1)} copy(bf16[64,576]{1,0:T(8,128)(2,1)} %get-tuple-element.4) | data formatting | bytes 147456
  117.1 1.6 %copy.16 = bf16[16,4608]{1,0:T(8,128)(2,1)} copy(bf16[16,4608]{1,0:T(8,128)(2,1)} %get-tuple-element.5) | data formatting | bytes 294912

commit v2 on v1

v2 whole, which is shorter than its diff:
```python
import functools

import jax
import jax.numpy as jnp
from jax import lax
from jax.experimental import pallas as pl
from jax.experimental.pallas import tpu as pltpu
from jax.sharding import PartitionSpec as P

D = 18432
EPS = 1e-05
MESH = pl.DeviceIdType.MESH
F32 = jnp.float32
BF16 = jnp.bfloat16
KB = 576
KP = 640
CHUNKS = 9
CW = 256
HALF = CHUNKS * CW

STEP = dict(Q1=2, Q2=5, Q4=7, C1=8, C2=9, C4=11, C5=13)
LAG1, LAG2, LAG3 = 2, 4, 6
Z_LAG1, Z_LAG2 = 4, 7
Z_FIRST = (0,)
STEPS = 16


def device(x, y, zl, zh, c):
    return ((zl * 4 + x) * 2 + c, zh * 4 + y)


def kernel(
    hidden,
    gain,
    gate_w,
    up_w,
    query_w,
    kv_w,
    out_w,
    keys_h,
    values_h,
    lengths,
    update,
    slab,
    raw,
    normed,
    gains,
    wgu,
    wq,
    wkv,
    wo,
    keys,
    values,
    cst,
    zst,
    xst,
    yst,
    part,
    r1,
    s1,
    r2,
    zs,
    zr,
    zb,
    xs,
    xr,
    sl,
    sr,
    kvs,
    kvp,
    kvr,
    kz,
    kzr,
    kc,
    pq,
    rq,
    zq,
    zqr,
    cx,
    yt,
    yr,
    q48,
    ctx,
    caf,
    ca,
    ar,
    bs,
    br,
    brf,
    ctf,
    ct,
    os_,
    or_,
    vf,
    fs,
    fr,
    gs,
    gr,
    lsem,
    sent,
    come,
    chunk_w,
    chunk_1,
    chunk_2,
    chunk_3,
):
    w = lax.axis_index("wide")
    n = lax.axis_index("narrow")
    c = lax.rem(w, 2)
    x = lax.rem(w // 2, 4)
    zl = w // 8
    zh = n // 4
    y = lax.rem(n, 4)
    z = zh * 4 + zl
    oc = 1 - c
    sib = device(x, y, zl, zh, 1 - c)
    partner = device(x, y, zl, 1 - zh, c)
    partner_sib = device(x, y, zl, 1 - zh, oc)

    def on_x(p):
        return device(p, y, zl, zh, c)

    def on_y(p):
        return device(x, p, zl, zh, c)

    def on_y_sib(p):
        return device(x, p, zl, zh, oc)

    def on_z(p):
        return device(x, y, lax.rem(p, 4), p // 4, c)

    def remote(src, dst, ss, rs, to):
        return pltpu.make_async_remote_copy(
            src_ref=src, dst_ref=dst, send_sem=ss, recv_sem=rs, device_id=to, device_id_type=MESH
        )

    def peers(me, size):
        return [(d, lax.rem(me + d, size)) for d in range(1, size)]

    on_x.peers, on_y.peers, on_z.peers = peers(x, 4), peers(y, 4), peers(z, 8)
    zl_peers = peers(zl, 4)

    def on_zl(p):
        return device(x, y, p, zh, c)

    on_zl.peers = zl_peers

    names = (
        "cst", "zst", "xst", "yst", "gain", "near", "zh0", "zh1", "far0", "far1", "sib0", "sib1", "sib2", "wq", "wkv",
        "wo", "qx", "kx", "qz", "kz", "kc", "qy", "a", "b", "c", "e0", "e1", "f", "g",
        "last",
    )
    slot = {name: i for i, name in enumerate(names)}

    def start(name, src, dst, to):
        remote(src, dst, sent.at[slot[name]], come.at[slot[name]], to).start()

    def arrive(name, dst):
        remote(dst, dst, sent.at[slot[name]], come.at[slot[name]], sib).wait_recv()

    def spread(name, src, dst, me, on):
        for _, p in on.peers:
            start(name, src(p), dst.at[me], on(p))

    def collect(name, dst, on):
        arrive(name, dst.at[pl.ds(0, len(on.peers))])

    half = pl.multiple_of(c * HALF, 128)
    other = pl.multiple_of((1 - c) * HALF, 128)
    mine = pl.ds(pl.multiple_of(c * KP, 128), KB)

    def local(src, dst, i):
        return pltpu.make_async_copy(src, dst, lsem.at[i])

    load_x = local(hidden, raw.at[c, n], 0)
    load_x.start()
    load_q = local(query_w.at[:, pl.ds(pl.multiple_of(c * 384, 128), 384)], wq.at[mine], 1)
    load_kv = local(kv_w.at[:, pl.ds(pl.multiple_of(c * 256, 128), 256)], wkv.at[mine], 2)
    load_o = local(out_w, wo.at[c], 3)
    load_k = local(keys_h, keys, 4)
    load_v = local(values_h, values, 5)
    load_q.start()
    load_kv.start()

    barrier = pltpu.get_barrier_semaphore()
    greeted = [on(p) for on in (on_z, on_x, on_y) for _, p in on.peers] + [sib]
    greeted += [on_y_sib(p) for _, p in on_y.peers] + [partner_sib]
    for to in greeted:
        pl.semaphore_signal(barrier, inc=1, device_id=to, device_id_type=MESH)

    for k in range(2):
        pad = pl.ds(k * KP + KB, KP - KB)
        normed[:, pad] = jnp.zeros((512, KP - KB), BF16)
        wq[pad, :] = jnp.zeros((KP - KB, 384), BF16)
        wkv[pad, :] = jnp.zeros((KP - KB, 256), BF16)

        def fill(j, carry, pad=pad):
            wgu[j, pad, :] = jnp.zeros((KP - KB, 2 * CW), BF16)
            return carry

        lax.fori_loop(0, CHUNKS, fill, 0)
    caf[...] = jnp.zeros((2, 32, 256), F32)
    yt[...] = jnp.zeros((2, 4, 8, 384), F32)
    load_x.wait()
    own = raw[c, n].astype(F32)
    row64 = lax.broadcasted_iota(jnp.int32, (64, 128), 0)
    lane = lax.broadcasted_iota(jnp.int32, (64, 128), 1)
    both = jnp.where(
        lane < 64,
        jnp.sum(own, axis=1, keepdims=True),
        jnp.sum(own * own, axis=1, keepdims=True),
    )
    line = jnp.sum(jnp.where((lane & 63) == row64, both, 0.0), axis=0, keepdims=True)
    cst[c] = jnp.broadcast_to(line, (8, 128))
    gains[c] = jnp.broadcast_to(gain[...].reshape(1, KB), (8, KB))

    pl.semaphore_wait(barrier, len(greeted))

    start("cst", cst.at[c], cst.at[c], sib)
    top = [pl.ds(0, 32), pl.ds(32, 32)]
    for i in range(2):
        start(f"zh{i}", raw.at[c, n, top[i]], raw.at[c, n, top[i]], partner)
    for _, p in on_y.peers:
        start("near", raw.at[c, n], raw.at[c, n], on_y(p))
    start("gain", gains.at[c], gains.at[c], sib)
    arrive("cst", cst.at[oc])
    zst[z] = cst[0] + cst[1]
    spread("zst", lambda p: zst.at[z], zst, z, on_z)
    away_q = pl.ds(pl.multiple_of((1 - c) * 384, 128), 384)
    away_kv = pl.ds(pl.multiple_of((1 - c) * 256, 128), 256)
    start("wq", query_w.at[:, away_q], wq.at[mine], sib)
    start("wkv", kv_w.at[:, away_kv], wkv.at[mine], sib)

    def start_weights(j, carry):
        g = j // 3
        for k, weight in enumerate((gate_w, up_w)):
            to = wgu.at[j, mine, pl.ds(k * CW, CW)]
            there = weight.at[:, pl.ds(pl.multiple_of(other + j * CW, 128), CW)]
            remote(there, to, chunk_w.at[0], chunk_w.at[1 + g], sib).start()
            here = weight.at[:, pl.ds(pl.multiple_of(half + j * CW, 128), CW)]
            local(here, to, 6 + g).start()
        return carry

    lax.fori_loop(0, CHUNKS, start_weights, 0)
    start("wo", out_w, wo.at[c], sib)
    load_o.start()
    load_k.start()
    load_v.start()

    far = (1 - zh) * 4 + y
    near4 = pl.ds(zh * 4, 4)
    far4 = pl.ds((1 - zh) * 4, 4)
    collect("zst", zst, on_z)
    upper = lax.broadcasted_iota(jnp.int32, (8, 128), 0) < 4
    xst[x] = jnp.where(
        upper, (zst[0] + zst[1]) + (zst[2] + zst[3]), (zst[4] + zst[5]) + (zst[6] + zst[7])
    )
    spread("xst", lambda p: xst.at[x], xst, x, on_x)
    for i in range(2):
        arrive(f"zh{i}", raw.at[c, far, top[i]])
        for _, p in on_y.peers:
            start(f"far{i}", raw.at[c, far, top[i]], raw.at[c, far, top[i]], on_y(p))
    arrive("near", raw.at[c, pl.ds(0, 3)])
    start("sib0", raw.at[c, near4], raw.at[c, near4], sib)
    collect("xst", xst, on_x)
    yst[y] = (xst[0] + xst[1]) + (xst[2] + xst[3])
    spread("yst", lambda p: yst.at[y], yst, y, on_y)
    def far_rows():
        for i in range(2):
            arrive(f"far{i}", raw.at[c, pl.ds(0, 3), top[i]])
            start(f"sib{i + 1}", raw.at[c, far4, top[i]], raw.at[c, far4, top[i]], sib)
        for i in range(2):
            arrive(f"sib{i + 1}", raw.at[oc, far4, top[i]])

    def norm(i, carry):
        b = lax.rem(i + zh * 4, 8)
        tile = yst[lax.rem(b, 4)]
        stat = jnp.where(b < 4, tile[0:1, :], tile[4:5, :])

        def column(at):
            return jnp.sum(jnp.where(lane == row64 + at, stat, 0.0), axis=1, keepdims=True)

        average = column(0) / D
        variance = column(64) / D - average * average
        scale = lax.rsqrt(variance + EPS)
        rows = pl.ds(pl.multiple_of(b * 64, 64), 64)
        for k in range(2):
            block = (raw[k, b].astype(F32) - average) * scale * gains[k, 0:1, :]
            normed[rows, k * KP : k * KP + KB] = block.astype(BF16)
        return carry

    load_q.wait()
    load_kv.wait()
    arrive("wq", wq.at[mine])
    arrive("wkv", wkv.at[mine])
    for i in range(2):
        if i == 0:
            arrive("gain", gains.at[oc])
            collect("yst", yst, on_y)
            arrive("sib0", raw.at[oc, near4])
        else:
            far_rows()
        lax.fori_loop(4 * i, 4 * i + 4, norm, 0)
        side = zh if i == 0 else 1 - zh
        rows = normed[pl.ds(pl.multiple_of(side * 256, 256), 256), :]
        query = jnp.dot(rows, wq[...], preferred_element_type=F32)
        for zz in range(2):
            for xx in range(4):
                at = zz * 128 + xx * 32
                pq[xx, side * 2 + zz] = query[at : at + 32]
        two = pl.ds(side * 2, 2)
        for _, p in on_x.peers:
            start("qx", pq.at[p, two], rq.at[x, two], on_x(p))
    k64 = lax.broadcasted_iota(jnp.int32, (64, 512), 0)
    r512 = lax.broadcasted_iota(jnp.int32, (64, 512), 1)
    pick = r512 == (k64 >> 1) * 16 + n * 2 + (k64 & 1)
    chosen = jnp.dot(
        jnp.where(pick, 1.0, 0.0).astype(BF16), normed[...], preferred_element_type=F32
    ).astype(BF16)
    kvs[...] = jnp.dot(chosen, wkv[...], preferred_element_type=F32)
    for zz in range(4):
        for xx in range(4):
            at = zz * 16 + xx * 4
            kvp[xx, zz, 0:4, :] = kvs[at : at + 4, 0:128]
            kvp[xx, zz, 4:8, :] = kvs[at : at + 4, 128:256]
    spread("kx", lambda p: kvp.at[p], kvr, x, on_x)

    def part_q1():
        collect("qx", rq, on_x)
        total = pq[x]
        for _, p in on_x.peers:
            total = total + rq[p]
        for zz in range(4):
            for hh in range(2):
                to = hh * 4 + zz
                zq[to, 0:8] = total[zz, hh * 8 : hh * 8 + 8]
                zq[to, 8:16] = total[zz, 16 + hh * 8 : 24 + hh * 8]
        zqr[z] = zq[z]
        spread("qz", lambda p: zq.at[p], zqr, z, on_z)
        collect("kx", kvr, on_x)
        fresh = kvp[x]
        for _, p in on_x.peers:
            fresh = fresh + kvr[p]
        kz[...] = fresh
        spread("kz", lambda p: kz.at[p], kzr, zl, on_zl)

    def part_q2():
        collect("qz", zqr, on_z)
        sums = [(zqr[k] + zqr[k + 1]) + (zqr[k + 2] + zqr[k + 3]) for k in (0, 4)]
        for hh in range(2):
            cx[hh] = sums[hh]
        for cc in range(2):
            for yy in range(4):
                for hh in range(2):
                    at = cc * 8 + yy * 2
                    yt[cc, yy, hh * 2 : hh * 2 + 2, :] = cx[hh, at : at + 2, :]
        here = c * 4 + y
        yr[here] = yt[c, y]
        for _, p in on_y.peers:
            start("qy", yt.at[c, p], yr.at[here], on_y(p))
            start("qy", yt.at[oc, p], yr.at[here], on_y_sib(p))
        start("qy", yt.at[oc, y], yr.at[here], sib)
        collect("kz", kzr, on_zl)
        fresh = kz[zl]
        for _, p in zl_peers:
            fresh = fresh + kzr[p]
        kc[c] = fresh
        start("kc", kc.at[c], kc.at[c], sib)

    def part_q4():
        arrive("kc", kc.at[oc])
        arrive("qy", yr.at[pl.ds(0, 7)])
        for yy in range(4):
            at = yy * 4
            q48[at : at + 4, :] = yr[yy, 0:4, 0:256]
            q48[16 + at : 20 + at, 0:128] = yr[yy, 0:4, 256:384]
            q48[16 + at : 20 + at, 128:256] = yr[4 + yy, 0:4, 0:128]
            q48[32 + at : 36 + at, :] = yr[4 + yy, 0:4, 128:384]
        load_k.wait()
        load_v.wait()
        q = q48[...].astype(BF16)
        factor = 1.0 / 16.0
        first = lax.broadcasted_iota(jnp.int32, (48, 1), 0) % 2 == 0

        def fresh(k):
            tile = kc[k].astype(BF16).astype(F32)
            sides = []
            for at in (0, 4):
                pair = jnp.where(c == 0, tile[at : at + 2], tile[at + 2 : at + 4])
                sides.append(jnp.where(first, pair[0:1, :], pair[1:2, :]))
            return jnp.concatenate(sides, axis=1)

        def scores_of(r):
            return lax.dot_general(q, keys[r], (((1,), (1,)), ((), ())), preferred_element_type=F32)

        scores = jnp.where(first, scores_of(0), scores_of(1)) * factor
        own_score = jnp.sum(q.astype(F32) * fresh(0), axis=1, keepdims=True) * factor
        position = lax.broadcasted_iota(jnp.int32, (48, 384), 1)
        usable = position < jnp.where(first, lengths[0], lengths[1])
        masked = jnp.where(usable, scores, -1e30)
        highest = jnp.maximum(jnp.max(masked, axis=1, keepdims=True), own_score)
        exps = jnp.where(usable, jnp.exp(masked - highest), 0.0)
        own_exp = jnp.exp(own_score - highest)
        denominator = jnp.sum(exps, axis=1, keepdims=True) + own_exp
        weights = (exps / denominator).astype(BF16)
        own_weight = (own_exp / denominator).astype(BF16).astype(F32)

        def mixed(r):
            return jnp.dot(weights, values[r], preferred_element_type=F32)

        context = jnp.where(first, mixed(0), mixed(1)) + own_weight * fresh(1)
        ctx[...] = context
        for t in range(3):
            for yy in range(4):
                for hh in range(2):
                    at = t * 16 + yy * 4 + hh * 2
                    caf[hh, yy * 8 + t * 2 : yy * 8 + t * 2 + 2, :] = ctx[at : at + 2, :]
        ca[...] = caf[...].astype(BF16)
        ar[z] = ca[zh]
        spread("a", lambda p: ca.at[p // 4], ar, z, on_z)

    def part_c1():
        collect("a", ar, on_z)
        for yy in range(4):
            bs[yy] = ar[:, yy * 8 : yy * 8 + 8, :].astype(F32).reshape(64, 256).astype(BF16)
        br[y] = bs[y]
        spread("b", lambda p: bs.at[p], br, y, on_y)

    def part_c2():
        collect("b", br, on_y)
        brf[...] = br[...].astype(F32)
        for t in range(3):
            for zz in range(4):
                for hh in range(2):
                    for yy in range(4):
                        to = zz * 16 + hh * 8 + yy * 2
                        at = (hh * 4 + zz) * 8 + t * 2
                        ctf[to : to + 2, t * 256 : t * 256 + 256] = brf[yy, at : at + 2, :]
        ct[x] = ctf[...].astype(BF16)
        for _, p in on_x.peers:
            start("c", ct.at[x], ct.at[x], on_x(p))

    def part_c4():
        load_o.wait()
        arrive("wo", wo.at[oc])
        collect("c", ct, on_x)
        for cc in range(2):
            out = lax.dot_general(
                ct[...].reshape(256, 768),
                wo[cc],
                (((1,), (1,)), ((), ())),
                preferred_element_type=F32,
            )
            for xx in range(4):
                for zz in range(4):
                    at = xx * 64 + zz * 16
                    to = (xx % 2) * 16
                    i = jnp.where(zh == zz // 2, 1, 0)
                    block = out[at : at + 16].astype(BF16)
                    os_[i, (zz % 2) * 2 + xx // 2, cc, to : to + 16, :] = block
        for i in range(2):
            spread(f"e{i}", lambda p, i=i: os_.at[i, p], or_.at[i], y, on_y)

    def summed(i):
        collect(f"e{i}", or_.at[i], on_y)
        total = os_[i, y].astype(F32)
        for _, p in on_y.peers:
            total = total + or_[i, p].astype(F32)
        return total

    def part_c5():
        fs[...] = summed(0).astype(BF16)
        start("f", fs.at[c], fr.at[0], partner)
        start("f", fs.at[oc], fr.at[1], partner_sib)
        vf[...] = summed(1)
        gs[...] = vf[oc].astype(BF16)
        start("g", gs, gr, sib)

    right, left = lax.rem(x + 1, 4), lax.rem(x + 3, 4)
    across = lax.rem(x + 2, 4)

    def first_copies(j):
        for k, to in enumerate((right, left)):
            src = part.at[j, :, across, :, pl.ds(k * CW, CW)]
            remote(src, r1.at[j, k], chunk_1.at[0], chunk_1.at[1 + j], on_x(to)).start()

    def came(sems, j, dst):
        remote(dst, dst, sems.at[0], sems.at[1 + j], sib).wait_recv()

    def z_first(j):
        return functools.reduce(jnp.logical_or, [j == b for b in Z_FIRST])

    def z_index(j):
        return sum([jnp.where(j > b, 1, 0) for b in Z_FIRST[:-1]], 0)

    def multiply(j):
        def ready():
            three = pl.ds(j, 3)
            to = wgu.at[three, mine]
            local(to, to, 6 + j // 3).wait()
            remote(to, to, chunk_w.at[0], chunk_w.at[1 + j // 3], sib).wait_recv()

        pl.when(lax.rem(j, 3) == 0)(ready)
        product = jnp.dot(normed[...], wgu[j], preferred_element_type=F32)
        part[j] = product.astype(BF16).reshape(4, 4, 32, 2 * CW)

        @pl.when(jnp.logical_not(z_first(j)))
        def _():
            first_copies(j)

        @pl.when(z_first(j))
        def _():
            for _, p in zl_peers:
                to = zb.at[z_index(j), zl]
                remote(part.at[j, p], to, chunk_1.at[0], chunk_1.at[1 + j], on_zl(p)).start()

    def add_first(j):
        came(chunk_1, j, r1.at[j])
        for k, to in enumerate((right, left)):
            for m in range(2):
                cols = slice(m * CW, m * CW + CW)
                if m == k:
                    total = part[j, :, to, :, cols].astype(F32) + r1[j, k].astype(F32)
                    s1[j, k, :, :, cols] = total.astype(BF16)
                else:
                    s1[j, k, :, :, cols] = part[j, :, to, :, cols]
            remote(s1.at[j, k], r2.at[j, k], chunk_2.at[0], chunk_2.at[1 + j], on_x(to)).start()

    def add_second(j):
        came(chunk_2, j, r2.at[j])
        total = part[j, :, x].astype(F32) + r2[j, 0].astype(F32) + r2[j, 1].astype(F32)
        zs[j] = total.astype(BF16)
        for _, p in zl_peers:
            remote(zs.at[j, p], zr.at[j, zl], chunk_3.at[0], chunk_3.at[1 + j], on_zl(p)).start()

    def add_z(j):
        i = z_index(j)
        came(chunk_1, j, zb.at[i, pl.ds(0, 3)])
        total = part[j, zl].astype(F32)
        for _, p in zl_peers:
            total = total + zb[i, p].astype(F32)
        xs[i] = total.astype(BF16)
        for _, p in on_x.peers:
            remote(xs.at[i, p], xr.at[i, x], chunk_2.at[0], chunk_2.at[1 + j], on_x(p)).start()

    def gated(j, total):
        g = total[:, :CW]
        hidden_units = (g * (1.0 / (1.0 + jnp.exp(-g))) * total[:, CW:]).astype(BF16)
        sl[j] = hidden_units.reshape(2, 16, CW)
        start("last", sl.at[j, 1 - c], sr.at[j], sib)
        slab[:, pl.ds(pl.multiple_of(half + j * CW, 128), CW)] = sl[j, c]

    def finish(j):
        came(chunk_3, j, zr.at[j, pl.ds(0, 3)])
        total = zs[j, zl].astype(F32)
        for _, p in zl_peers:
            total = total + zr[j, p].astype(F32)
        gated(j, total)

    def finish_z(j):
        i = z_index(j)
        came(chunk_2, j, xr.at[i, pl.ds(0, 3)])
        total = xs[i, x].astype(F32)
        for _, p in on_x.peers:
            total = total + xr[i, p].astype(F32)
        gated(j, total)

    parts = dict(
        Q1=part_q1, Q2=part_q2, Q4=part_q4, C1=part_c1, C2=part_c2, C4=part_c4, C5=part_c5
    )

    def step(k, carry):
        for name, run in parts.items():
            pl.when(k == STEP[name])(run)
        for lag, run, z_kind in (
            (LAG3, finish, False),
            (Z_LAG2, finish_z, True),
            (LAG2, add_second, False),
            (Z_LAG1, add_z, True),
            (LAG1, add_first, False),
            (0, multiply, None),
        ):
            j = k - lag
            due = jnp.logical_and(j >= 0, j < CHUNKS)
            if z_kind is not None:
                due = jnp.logical_and(due, z_first(j) == z_kind)
            pl.when(due)(functools.partial(run, j))
        return carry

    lax.fori_loop(0, STEPS, step, 0)

    arrive("last", sr)

    def rest(j, carry):
        slab[:, pl.ds(pl.multiple_of(other + j * CW, 128), CW)] = sr[j]
        return carry

    lax.fori_loop(0, CHUNKS, rest, 0)
    arrive("f", fr)
    arrive("g", gr)
    for core, total in ((c, vf[c] + fr[0].astype(F32)), (oc, gr[...].astype(F32) + fr[1].astype(F32))):
        for xx in range(2):
            rows = pl.ds(pl.multiple_of(xx * 32 + core * 16, 16), 16)
            update[rows, :] = total[xx * 16 : xx * 16 + 16].astype(BF16)

    of3, of7 = pl.ds(0, 3), pl.ds(0, 7)
    left_bytes = dict(
        cst=cst.at[0], zst=zst.at[of7], xst=xst.at[of3], yst=yst.at[of3], gain=gains.at[0],
        near=raw.at[0, of3], zh0=raw.at[0, 0, top[0]], zh1=raw.at[0, 0, top[0]],
        far0=raw.at[0, of3, top[0]], far1=raw.at[0, of3, top[0]], sib0=raw.at[0, pl.ds(0, 4)],
        sib1=raw.at[0, pl.ds(0, 4), top[0]], sib2=raw.at[0, pl.ds(0, 4), top[0]], wq=wq.at[pl.ds(0, KB)], wkv=wkv.at[pl.ds(0, KB)],
        qx=rq.at[of3], kx=kvr.at[of3], qz=zqr.at[of7], kz=kzr.at[of3], kc=kc.at[0], wo=wo.at[0],
        qy=yr.at[of7], a=ar.at[of7], b=br.at[of3], c=ct.at[of3],
        e0=or_.at[0, of3], e1=or_.at[1, of3], f=fr, g=gr, last=sr,
    )
    for name, dst in left_bytes.items():
        remote(dst, dst, sent.at[slot[name]], come.at[slot[name]], sib).wait_send()

    def gone(sems, dst):
        remote(dst, dst, sems.at[0], sems.at[1], sib).wait_send()

    a_kind, b_kind = pl.ds(0, CHUNKS - len(Z_FIRST)), pl.ds(0, len(Z_FIRST))
    gone(chunk_w, wgu.at[:, mine])
    gone(chunk_1, r1.at[a_kind])
    gone(chunk_1, zb.at[:, pl.ds(0, 3)])
    gone(chunk_2, r2.at[a_kind])
    gone(chunk_2, xr.at[:, pl.ds(0, 3)])
    gone(chunk_3, zr.at[a_kind, pl.ds(0, 3)])


def scratch():
    v = pltpu.VMEM
    z_chunks = len(Z_FIRST)
    buffers = [
        v((2, 8, 64, KB), BF16),
        v((512, 2 * KP), BF16),
        v((2, 8, KB), F32),
        v((CHUNKS, 2 * KP, 2 * CW), BF16),
        v((2 * KP, 384), BF16),
        v((2 * KP, 256), BF16),
        v((2, KB, 768), BF16),
        v((2, 384, 256), BF16),
        v((2, 384, 256), BF16),
        v((2, 8, 128), F32),
        v((8, 8, 128), F32),
        v((4, 8, 128), F32),
        v((4, 8, 128), F32),
        v((CHUNKS, 4, 4, 32, 2 * CW), BF16),
        v((CHUNKS, 2, 4, 32, CW), BF16),
        v((CHUNKS, 2, 4, 32, 2 * CW), BF16),
        v((CHUNKS, 2, 4, 32, 2 * CW), BF16),
        v((CHUNKS, 4, 32, 2 * CW), BF16),
        v((CHUNKS, 4, 32, 2 * CW), BF16),
        v((z_chunks, 4, 4, 32, 2 * CW), BF16),
        v((z_chunks, 4, 32, 2 * CW), BF16),
        v((z_chunks, 4, 32, 2 * CW), BF16),
        v((CHUNKS, 2, 16, CW), BF16),
        v((CHUNKS, 16, CW), BF16),
        v((64, 256), F32),
        v((4, 4, 8, 128), F32),
        v((4, 4, 8, 128), F32),
        v((4, 8, 128), F32),
        v((4, 8, 128), F32),
        v((2, 8, 128), F32),
        v((4, 4, 32, 384), F32),
        v((4, 4, 32, 384), F32),
        v((8, 16, 384), F32),
        v((8, 16, 384), F32),
        v((2, 16, 384), F32),
        v((2, 4, 8, 384), F32),
        v((8, 8, 384), F32),
        v((48, 256), F32),
        v((48, 256), F32),
        v((2, 32, 256), F32),
        v((2, 32, 256), BF16),
        v((8, 32, 256), BF16),
        v((4, 64, 256), BF16),
        v((4, 64, 256), BF16),
        v((4, 64, 256), F32),
        v((64, 768), F32),
        v((4, 64, 768), BF16),
        v((2, 4, 2, 32, KB), BF16),
        v((2, 4, 2, 32, KB), BF16),
        v((2, 32, KB), F32),
        v((2, 32, KB), BF16),
        v((2, 32, KB), BF16),
        v((32, KB), BF16),
        v((32, KB), BF16),
    ]
    counts = (9, 30, 30, 4, 1 + CHUNKS, 1 + CHUNKS, 1 + CHUNKS)
    return buffers + [pltpu.SemaphoreType.DMA((count,)) for count in counts]


def copy_out(update, slab, update_out, slab_out):
    update_out[...] = update[...]
    slab_out[...] = slab[...]


def local(hidden, gain, gate_w, up_w, query_w, kv_w, out_w, *rest):
    anywhere = pl.BlockSpec(memory_space=pl.ANY)
    vmem = pl.BlockSpec(memory_space=pltpu.VMEM)
    shapes = (
        jax.ShapeDtypeStruct((64, KB), BF16),
        jax.ShapeDtypeStruct((16, 2 * HALF), BF16),
    )
    results = pl.pallas_call(
        kernel,
        out_shape=shapes,
        in_specs=[anywhere, vmem] + [anywhere] * 7 + [pl.BlockSpec(memory_space=pltpu.SMEM)],
        out_specs=(vmem, vmem),
        scratch_shapes=scratch(),
        compiler_params=pltpu.CompilerParams(
            collective_id=0, has_side_effects=True, vmem_limit_bytes=58 * 1024 * 1024
        ),
        name="layer",
    )(hidden, gain, gate_w, up_w, query_w, kv_w, out_w.T, *rest)
    return pl.pallas_call(
        copy_out,
        out_shape=shapes,
        in_specs=[vmem, vmem],
        out_specs=(vmem, vmem),
        name="outputs",
    )(*results)


def solution(mesh):
    placed = (
        P("narrow", "wide"),
        P("wide"),
        P("wide", "narrow"),
        P("wide", "narrow"),
        P("wide", "narrow"),
        P("wide", None),
        P("narrow", "wide"),
        P(("wide", "narrow"), None, None),
        P(("wide", "narrow"), None, None),
        P(("wide", "narrow")),
    )
    return jax.shard_map(
        local,
        mesh=mesh,
        in_specs=placed,
        out_specs=(P("narrow", "wide"), P("wide", "narrow")),
        check_vma=False,
    )
```

time: 119 us -> 92.7 us (0.78)
  Pallas kernels: 111 us -> 91.9 us
  local copies, waits for them, and re-layouts: 6.6 us -> 0 us
    pallas_call x1 -> x2, Pallas kernels: 111 us -> 91.9 us  [the longest x1 90.3 us: local(): pl.pallas_call(kernel, out_shape=shapes, in_specs=[anywhere, vmem] + [any...]
    unnamed x3 -> x0, local copies, waits for them, and re-layouts: 5.34 us -> none
    reshape x1 -> x0, local copies, waits for them, and re-layouts: 1.27 us -> none  [local(): gain.reshape(1, KB)]
where the time goes in v2:
time: 92.7 us; the launch traced here: 92.6 us
  Pallas kernels  91.9 us (99%)
    pallas_call x1, Pallas kernels, local(): pl.pallas_call(kernel, out_shape=shapes, in_specs=[anywhere, vmem] + [any...  90.3 us

profile of v2, /device:TPU:1, one launch (start us, length us, event | category | flops | bytes accessed | tf_op | source)
XLA Modules:
  0.0 92.6 jit_solution(6143775850667618044)
XLA Ops:
  0.6 90.3 %layer.1 = (bf16[64,576]{1,0:T(8,128)(2,1)}, bf16[16,4608]{1,0:T(8,128)(2,1)}) custom-call(bf16[64,576]{1,0:T(8,128)(2,1)} %hidden.1, f32[576]{0:T(1024)} %gain.1, bf16[576,4608]{1,0:T(8,128)(2,1)} %gate_w.1, bf16[576,4608]{1,0:T(8,128)(2,1)} %up_w.1, bf16[576,768]{1,0:T(8,128)(2,1)} %query_w.1, bf16[576,512]{1,0:T(8,128)(2,1)} %kv_w.1, ...), custom_call_target="tpu_custom_call" | custom-call | tf_op jit(solution)/shard_map/layer/pallas_call | solution.py:706
  90.9 1.6 %outputs.1 = (bf16[64,576]{1,0:T(8,128)(2,1)}, bf16[16,4608]{1,0:T(8,128)(2,1)}) custom-call(bf16[64,576]{1,0:T(8,128)(2,1)} %get-tuple-element.4.update, bf16[16,4608]{1,0:T(8,128)(2,1)} %get-tuple-element.5.slab), custom_call_target="tpu_custom_call" | custom-call | tf_op jit(solution)/shard_map/outputs/pallas_call | solution.py:717

commit v3 on v2

--- a/solution.py
+++ b/solution.py
@@ -573,12 +573,12 @@
         for name, run in parts.items():
             pl.when(k == STEP[name])(run)
         for lag, run, z_kind in (
+            (0, multiply, None),
+            (LAG1, add_first, False),
             (LAG3, finish, False),
             (Z_LAG2, finish_z, True),
             (LAG2, add_second, False),
             (Z_LAG1, add_z, True),
-            (LAG1, add_first, False),
-            (0, multiply, None),
         ):
             j = k - lag
             due = jnp.logical_and(j >= 0, j < CHUNKS)

time: 92.7 us -> 91.9 us (level)
  no operation moved by 1% of the time
where the time goes in v3:
time: 91.9 us; the launch traced here: 91.7 us
  Pallas kernels  91.1 us (99%)
    pallas_call x1, Pallas kernels, local(): pl.pallas_call(kernel, out_shape=shapes, in_specs=[anywhere, vmem] + [any...  89.5 us

profile of v3, /device:TPU:1, one launch (start us, length us, event | category | flops | bytes accessed | tf_op | source)
XLA Modules:
  0.0 91.7 jit_solution(634573398275910296)
XLA Ops:
  0.6 89.5 %layer.1 = (bf16[64,576]{1,0:T(8,128)(2,1)}, bf16[16,4608]{1,0:T(8,128)(2,1)}) custom-call(bf16[64,576]{1,0:T(8,128)(2,1)} %hidden.1, f32[576]{0:T(1024)} %gain.1, bf16[576,4608]{1,0:T(8,128)(2,1)} %gate_w.1, bf16[576,4608]{1,0:T(8,128)(2,1)} %up_w.1, bf16[576,768]{1,0:T(8,128)(2,1)} %query_w.1, bf16[576,512]{1,0:T(8,128)(2,1)} %kv_w.1, ...), custom_call_target="tpu_custom_call" | custom-call | tf_op jit(solution)/shard_map/layer/pallas_call | solution.py:706
  90.1 1.6 %outputs.1 = (bf16[64,576]{1,0:T(8,128)(2,1)}, bf16[16,4608]{1,0:T(8,128)(2,1)}) custom-call(bf16[64,576]{1,0:T(8,128)(2,1)} %get-tuple-element.4.update, bf16[16,4608]{1,0:T(8,128)(2,1)} %get-tuple-element.5.slab), custom_call_target="tpu_custom_call" | custom-call | tf_op jit(solution)/shard_map/outputs/pallas_call | solution.py:717

commit v4 on v3

--- a/solution.py
+++ b/solution.py
@@ -19,7 +19,7 @@
 HALF = CHUNKS * CW
 
 STEP = dict(Q1=2, Q2=5, Q4=7, C1=8, C2=9, C4=11, C5=13)
-LAG1, LAG2, LAG3 = 2, 4, 6
+LAG1, LAG2, LAG3 = 2, 4, 7
 Z_LAG1, Z_LAG2 = 4, 7
 Z_FIRST = (0,)
 STEPS = 16

time: 91.9 us -> 91.9 us (level)
  no operation moved by 1% of the time
where the time goes in v4:
time: 91.9 us; the launch traced here: 91.7 us
  Pallas kernels  91.1 us (99%)
    pallas_call x1, Pallas kernels, local(): pl.pallas_call(kernel, out_shape=shapes, in_specs=[anywhere, vmem] + [any...  89.5 us

profile of v4, /device:TPU:1, one launch (start us, length us, event | category | flops | bytes accessed | tf_op | source)
XLA Modules:
  0.0 91.7 jit_solution(8734652348406309377)
XLA Ops:
  0.6 89.5 %layer.1 = (bf16[64,576]{1,0:T(8,128)(2,1)}, bf16[16,4608]{1,0:T(8,128)(2,1)}) custom-call(bf16[64,576]{1,0:T(8,128)(2,1)} %hidden.1, f32[576]{0:T(1024)} %gain.1, bf16[576,4608]{1,0:T(8,128)(2,1)} %gate_w.1, bf16[576,4608]{1,0:T(8,128)(2,1)} %up_w.1, bf16[576,768]{1,0:T(8,128)(2,1)} %query_w.1, bf16[576,512]{1,0:T(8,128)(2,1)} %kv_w.1, ...), custom_call_target="tpu_custom_call" | custom-call | tf_op jit(solution)/shard_map/layer/pallas_call | solution.py:706
  90.1 1.6 %outputs.1 = (bf16[64,576]{1,0:T(8,128)(2,1)}, bf16[16,4608]{1,0:T(8,128)(2,1)}) custom-call(bf16[64,576]{1,0:T(8,128)(2,1)} %get-tuple-element.4.update, bf16[16,4608]{1,0:T(8,128)(2,1)} %get-tuple-element.5.slab), custom_call_target="tpu_custom_call" | custom-call | tf_op jit(solution)/shard_map/outputs/pallas_call | solution.py:717
